TPU v7x, 32 devices: a whole 2x2x4 slice. The times are simulated.
32 devices in a mesh: dp: 8 (over z, x), shard: 4 (over y, core).
Axes of the slice: x: 2, y: 2, z: 4, core: 2. Of those that a mesh axis runs over, the one named last changes fastest.
Arguments:
- hidden_in: bfloat16 [8192, 1024], P(('dp', 'shard')), may hold values from -6 to 6
- memory: bfloat16 [16384, 1024], P(('dp', 'shard')), may hold values from -6 to 6
- dec_lengths: int32 [64], P(('dp', 'shard')), may hold values from 16 to 128, as said below
- mem_lengths: int32 [64], P(('dp', 'shard')), may hold values from 64 to 256, as said below
- cotangent: bfloat16 [8192, 1024], P(('dp', 'shard')), may hold values from -6 to 6
- self_project: bfloat16 [1024, 3072], P(('dp', 'shard')), may hold values from -0.1875 to 0.1875
- self_output: bfloat16 [1024, 1024], P(('dp', 'shard')), may hold values from -1.5 to 1.5
- cross_query: bfloat16 [1024, 1024], P(('dp', 'shard')), may hold values from -0.1875 to 0.1875
- cross_memory: bfloat16 [1024, 2048], P(('dp', 'shard')), may hold values from -0.1875 to 0.1875
- cross_output: bfloat16 [1024, 1024], P(('dp', 'shard')), may hold values from -1.5 to 1.5
- feed_in: bfloat16 [1024, 4096], P(('dp', 'shard')), may hold values from -0.1875 to 0.1875
- feed_out: bfloat16 [4096, 1024], P(('dp', 'shard')), may hold values from -0.1875 to 0.1875
- bias_rows: bfloat16 [7, 1024], P(None, ('dp', 'shard')), may hold values from -2 to 2
- feed_bias: bfloat16 [4096], P(('dp', 'shard')), may hold values from -2 to 2
- norm_gains: bfloat16 [3, 1024], P(None, ('dp', 'shard')), may hold values from 0.5 to 1.5
- norm_shifts: bfloat16 [3, 1024], P(None, ('dp', 'shard')), may hold values from -2 to 2
Outputs:
- block_out: bfloat16 [8192, 1024], P(('dp', 'shard'))
- grad_hidden: bfloat16 [8192, 1024], P(('dp', 'shard'))
- grad_memory: bfloat16 [16384, 1024], P(('dp', 'shard'))
- grad_self_project: float32 [1024, 3072], P(('dp', 'shard'))
- grad_self_output: float32 [1024, 1024], P(('dp', 'shard'))
- grad_cross_query: float32 [1024, 1024], P(('dp', 'shard'))
- grad_cross_memory: float32 [1024, 2048], P(('dp', 'shard'))
- grad_cross_output: float32 [1024, 1024], P(('dp', 'shard'))
- grad_feed_in: float32 [1024, 4096], P(('dp', 'shard'))
- grad_feed_out: float32 [4096, 1024], P(('dp', 'shard'))
- grad_bias_rows: float32 [7, 1024], P(None, ('dp', 'shard'))
- grad_feed_bias: float32 [4096], P(('dp', 'shard'))
- grad_norm_gains: float32 [3, 1024], P(None, ('dp', 'shard'))
- grad_norm_shifts: float32 [3, 1024], P(None, ('dp', 'shard'))
Inputs may be any that keep to these rules, and one draw needn't show every extreme that they name: `dec_lengths`: at least one sequence has all 128 decoder tokens valid. `mem_lengths`: at least one sequence has all 256 memory tokens valid.
All inputs are finite; a program needn't handle non-finite values.
Results may differ from a plain program's by a relative error of at most 0.02.
Values may be sent and summed in bfloat16 or wider, within the bound.
A program may use at most 320 MiB of HBM per device.

v0:
```python
import math

import jax
import jax.numpy as jnp
from jax import lax
from jax.sharding import PartitionSpec as P

D = 1024
HEADS = 16
HEAD_DIM = 64
DEC = 128
MEM = 256


alpha_res = 300.0**0.25
epsilon = 1e-05
gelu_coef = math.sqrt(2.0 / math.pi)


def gelu_tanh(value):
    inner = gelu_coef * (value + 0.044715 * value * value * value)
    return 0.5 * value * (1.0 + jnp.tanh(inner))


def gelu_slope(value):
    inner = gelu_coef * (value + 0.044715 * value * value * value)
    tangent = jnp.tanh(inner)
    return 0.5 * (1.0 + tangent) + 0.5 * value * (1.0 - tangent * tangent) * gelu_coef * (
        1.0 + 3.0 * 0.044715 * value * value
    )


def product(rows_mat, weight):
    return jnp.dot(rows_mat, weight, preferred_element_type=jnp.float32)


def times_trans(rows_mat, weight):
    return jnp.einsum("tj,ij->ti", rows_mat, weight, preferred_element_type=jnp.float32)


def outer_sum(left_rows, right_rows):
    return jnp.einsum("ti,tj->ij", left_rows, right_rows, preferred_element_type=jnp.float32)


def column_total(rows_mat):
    return jnp.sum(rows_mat.astype(jnp.float32), 0)


def layer_norm(resid, gain, shift):
    center = resid - jnp.mean(resid, -1, keepdims=True)
    inv_dev = lax.rsqrt(jnp.mean(center * center, -1, keepdims=True) + epsilon)
    scaled = center * inv_dev
    return (scaled * gain + shift, scaled, inv_dev)


def norm_back(grad_out, scaled, inv_dev, gain):
    grad_scaled = grad_out * gain
    grad_resid = inv_dev * (
        grad_scaled
        - jnp.mean(grad_scaled, -1, keepdims=True)
        - scaled * jnp.mean(grad_scaled * scaled, -1, keepdims=True)
    )
    return (grad_resid, jnp.sum(grad_out * scaled, 0), jnp.sum(grad_out, 0))


def split_heads(matrix):
    return matrix.reshape(matrix.shape[0], HEADS, HEAD_DIM)


def merge_heads(tensor):
    return tensor.reshape(tensor.shape[0], D)


def scores_of(query_rows, key_rows, allowed):
    raw = jnp.einsum(
        "qhe,khe->hqk",
        split_heads(query_rows),
        split_heads(key_rows),
        preferred_element_type=jnp.float32,
    )
    return jnp.where(allowed[None], raw * HEAD_DIM ** (-0.5), -1000000000.0)


def attend(query_rows, key_rows, value_rows, allowed):
    scores = scores_of(query_rows, key_rows, allowed)
    top_score = jnp.max(scores, -1, keepdims=True)
    log_total = top_score + jnp.log(jnp.sum(jnp.exp(scores - top_score), -1, keepdims=True))
    probabilities = jnp.exp(scores - log_total).astype(jnp.bfloat16)
    mixed = jnp.einsum(
        "hqk,khe->qhe", probabilities, split_heads(value_rows), preferred_element_type=jnp.float32
    )
    return (merge_heads(mixed).astype(jnp.bfloat16), log_total)


def attend_back(query_rows, key_rows, value_rows, allowed, log_total, grad_mixed):
    probabilities = jnp.exp(scores_of(query_rows, key_rows, allowed) - log_total)
    grad_heads = split_heads(grad_mixed)
    grad_value = jnp.einsum(
        "hqk,qhe->khe",
        probabilities.astype(jnp.bfloat16),
        grad_heads,
        preferred_element_type=jnp.float32,
    )
    grad_probs = jnp.einsum(
        "qhe,khe->hqk", grad_heads, split_heads(value_rows), preferred_element_type=jnp.float32
    )
    grad_scores = probabilities * (
        grad_probs - jnp.sum(probabilities * grad_probs, -1, keepdims=True)
    )
    grad_raw = (grad_scores * HEAD_DIM ** (-0.5)).astype(jnp.bfloat16)
    grad_query = jnp.einsum(
        "hqk,khe->qhe", grad_raw, split_heads(key_rows), preferred_element_type=jnp.float32
    )
    grad_key = jnp.einsum(
        "hqk,qhe->khe", grad_raw, split_heads(query_rows), preferred_element_type=jnp.float32
    )
    return (
        merge_heads(grad_query).astype(jnp.bfloat16),
        merge_heads(grad_key).astype(jnp.bfloat16),
        merge_heads(grad_value).astype(jnp.bfloat16),
    )


def masks_for(dec_len, mem_len):
    row_ids = jnp.arange(DEC)
    valid_rows = (row_ids < dec_len)[:, None]
    causal = (row_ids[None, :] <= row_ids[:, None]) & (row_ids[None, :] < dec_len)
    mem_seen = jnp.broadcast_to((jnp.arange(MEM) < mem_len)[None, :], (DEC, MEM))
    return (valid_rows, causal, mem_seen)


def run_forward(weights, hidden, mem_rows, dec_len, mem_len):
    (
        self_project,
        self_output,
        cross_query,
        cross_memory,
        cross_output,
        feed_in,
        feed_out,
        bias_rows,
        feed_bias,
        norm_gains,
        norm_shifts,
    ) = weights
    bias_full = bias_rows.astype(jnp.float32)
    gain_full = norm_gains.astype(jnp.float32)
    shift_full = norm_shifts.astype(jnp.float32)
    valid_rows, causal, mem_seen = masks_for(dec_len, mem_len)
    projected = product(hidden, self_project)
    query_rows = (projected[:, :D] + bias_full[0]).astype(jnp.bfloat16)
    key_rows = projected[:, D : 2 * D].astype(jnp.bfloat16)
    value_rows = (projected[:, 2 * D :] + bias_full[1]).astype(jnp.bfloat16)
    mixed, log_one = attend(query_rows, key_rows, value_rows, causal)
    resid_one = alpha_res * hidden.astype(jnp.float32) + product(mixed, self_output) + bias_full[2]
    first, scaled_one, inv_one = layer_norm(resid_one, gain_full[0], shift_full[0])
    first = first.astype(jnp.bfloat16)
    cross_q = (product(first, cross_query) + bias_full[3]).astype(jnp.bfloat16)
    mem_proj = product(mem_rows, cross_memory)
    cross_k = mem_proj[:, :D].astype(jnp.bfloat16)
    cross_v = (mem_proj[:, D:] + bias_full[4]).astype(jnp.bfloat16)
    mixed_two, log_two = attend(cross_q, cross_k, cross_v, mem_seen)
    resid_two = (
        alpha_res * first.astype(jnp.float32) + product(mixed_two, cross_output) + bias_full[5]
    )
    second, scaled_two, inv_two = layer_norm(resid_two, gain_full[1], shift_full[1])
    second = second.astype(jnp.bfloat16)
    pre_act = product(second, feed_in) + feed_bias.astype(jnp.float32)
    active = gelu_tanh(pre_act).astype(jnp.bfloat16)
    resid_three = alpha_res * second.astype(jnp.float32) + product(active, feed_out) + bias_full[6]
    normed, scaled_three, inv_three = layer_norm(resid_three, gain_full[2], shift_full[2])
    block_out = jnp.where(valid_rows, normed, 0.0).astype(jnp.bfloat16)
    saved = (
        query_rows,
        key_rows,
        value_rows,
        log_one,
        mixed,
        scaled_one,
        inv_one,
        first,
        cross_q,
        cross_k,
        cross_v,
        log_two,
        mixed_two,
        scaled_two,
        inv_two,
        second,
        pre_act,
        active,
        scaled_three,
        inv_three,
    )
    return (saved, block_out)


def run_backward(weights, saved, hidden, mem_rows, cot_rows, dec_len, mem_len):
    (
        self_project,
        self_output,
        cross_query,
        cross_memory,
        cross_output,
        feed_in,
        feed_out,
        bias_rows,
        feed_bias,
        norm_gains,
        norm_shifts,
    ) = weights
    (
        query_rows,
        key_rows,
        value_rows,
        log_one,
        mixed,
        scaled_one,
        inv_one,
        first,
        cross_q,
        cross_k,
        cross_v,
        log_two,
        mixed_two,
        scaled_two,
        inv_two,
        second,
        pre_act,
        active,
        scaled_three,
        inv_three,
    ) = saved
    gain_full = norm_gains.astype(jnp.float32)
    valid_rows, causal, mem_seen = masks_for(dec_len, mem_len)
    grad_top = jnp.where(valid_rows, cot_rows.astype(jnp.float32), 0.0)
    grad_three, gain_three, shift_three = norm_back(grad_top, scaled_three, inv_three, gain_full[2])
    branch_three = grad_three.astype(jnp.bfloat16)
    grad_feed_out = outer_sum(active, branch_three)
    grad_pre = (times_trans(branch_three, feed_out) * gelu_slope(pre_act)).astype(jnp.bfloat16)
    grad_feed_in = outer_sum(second, grad_pre)
    grad_second = (alpha_res * grad_three + times_trans(grad_pre, feed_in)).astype(jnp.bfloat16)
    grad_two, gain_two, shift_two = norm_back(
        grad_second.astype(jnp.float32), scaled_two, inv_two, gain_full[1]
    )
    branch_two = grad_two.astype(jnp.bfloat16)
    grad_cross_output = outer_sum(mixed_two, branch_two)
    grad_mixed_two = times_trans(branch_two, cross_output).astype(jnp.bfloat16)
    grad_cq, grad_ck, grad_cv = attend_back(
        cross_q, cross_k, cross_v, mem_seen, log_two, grad_mixed_two
    )
    grad_mem_proj = jnp.concatenate([grad_ck, grad_cv], 1)
    grad_cross_memory = outer_sum(mem_rows, grad_mem_proj)
    grad_mem_rows = times_trans(grad_mem_proj, cross_memory).astype(jnp.bfloat16)
    grad_cross_query = outer_sum(first, grad_cq)
    grad_first = (alpha_res * grad_two + times_trans(grad_cq, cross_query)).astype(jnp.bfloat16)
    grad_one, gain_one, shift_one = norm_back(
        grad_first.astype(jnp.float32), scaled_one, inv_one, gain_full[0]
    )
    branch_one = grad_one.astype(jnp.bfloat16)
    grad_self_output = outer_sum(mixed, branch_one)
    grad_mixed = times_trans(branch_one, self_output).astype(jnp.bfloat16)
    grad_q, grad_k, grad_v = attend_back(
        query_rows, key_rows, value_rows, causal, log_one, grad_mixed
    )
    grad_projected = jnp.concatenate([grad_q, grad_k, grad_v], 1)
    grad_self_project = outer_sum(hidden, grad_projected)
    grad_hidden = (alpha_res * grad_one + times_trans(grad_projected, self_project)).astype(
        jnp.bfloat16
    )
    grad_bias_rows = jnp.stack(
        [
            column_total(grad_q),
            column_total(grad_v),
            column_total(branch_one),
            column_total(grad_cq),
            column_total(grad_cv),
            column_total(branch_two),
            column_total(branch_three),
        ]
    )
    grads = (
        grad_self_project,
        grad_self_output,
        grad_cross_query,
        grad_cross_memory,
        grad_cross_output,
        grad_feed_in,
        grad_feed_out,
        grad_bias_rows,
        column_total(grad_pre),
        jnp.stack([gain_one, gain_two, gain_three]),
        jnp.stack([shift_one, shift_two, shift_three]),
    )
    return (grads, grad_hidden, grad_mem_rows)


def fetch_forward(owned):
    return (
        lax.all_gather(owned[0], ("dp", "shard"), axis=0, tiled=True),
        lax.all_gather(owned[1], ("dp", "shard"), axis=0, tiled=True),
        lax.all_gather(owned[2], ("dp", "shard"), axis=0, tiled=True),
        lax.all_gather(owned[3], ("dp", "shard"), axis=0, tiled=True),
        lax.all_gather(owned[4], ("dp", "shard"), axis=0, tiled=True),
        lax.all_gather(owned[5], ("dp", "shard"), axis=0, tiled=True),
        lax.all_gather(owned[6], ("dp", "shard"), axis=0, tiled=True),
        lax.all_gather(owned[7], ("dp", "shard"), axis=1, tiled=True),
        lax.all_gather(owned[8], ("dp", "shard"), axis=0, tiled=True),
        lax.all_gather(owned[9], ("dp", "shard"), axis=1, tiled=True),
        lax.all_gather(owned[10], ("dp", "shard"), axis=1, tiled=True),
    )


def fetch_backward(owned):
    return (
        lax.all_gather(owned[0], ("dp", "shard"), axis=0, tiled=True),
        lax.all_gather(owned[1], ("dp", "shard"), axis=0, tiled=True),
        lax.all_gather(owned[2], ("dp", "shard"), axis=0, tiled=True),
        lax.all_gather(owned[3], ("dp", "shard"), axis=0, tiled=True),
        lax.all_gather(owned[4], ("dp", "shard"), axis=0, tiled=True),
        lax.all_gather(owned[5], ("dp", "shard"), axis=0, tiled=True),
        lax.all_gather(owned[6], ("dp", "shard"), axis=0, tiled=True),
        lax.all_gather(owned[7], ("dp", "shard"), axis=1, tiled=True),
        lax.all_gather(owned[8], ("dp", "shard"), axis=0, tiled=True),
        lax.all_gather(owned[9], ("dp", "shard"), axis=1, tiled=True),
        lax.all_gather(owned[10], ("dp", "shard"), axis=1, tiled=True),
    )


def share_each(grads):
    return (
        lax.psum_scatter(grads[0], ("dp", "shard"), scatter_dimension=0, tiled=True),
        lax.psum_scatter(grads[1], ("dp", "shard"), scatter_dimension=0, tiled=True),
        lax.psum_scatter(grads[2], ("dp", "shard"), scatter_dimension=0, tiled=True),
        lax.psum_scatter(grads[3], ("dp", "shard"), scatter_dimension=0, tiled=True),
        lax.psum_scatter(grads[4], ("dp", "shard"), scatter_dimension=0, tiled=True),
        lax.psum_scatter(grads[5], ("dp", "shard"), scatter_dimension=0, tiled=True),
        lax.psum_scatter(grads[6], ("dp", "shard"), scatter_dimension=0, tiled=True),
        lax.psum_scatter(grads[7], ("dp", "shard"), scatter_dimension=1, tiled=True),
        lax.psum_scatter(grads[8], ("dp", "shard"), scatter_dimension=0, tiled=True),
        lax.psum_scatter(grads[9], ("dp", "shard"), scatter_dimension=1, tiled=True),
        lax.psum_scatter(grads[10], ("dp", "shard"), scatter_dimension=1, tiled=True),
    )


def body(
    hidden_in,
    memory,
    dec_lengths,
    mem_lengths,
    cotangent,
    self_project,
    self_output,
    cross_query,
    cross_memory,
    cross_output,
    feed_in,
    feed_out,
    bias_rows,
    feed_bias,
    norm_gains,
    norm_shifts,
):
    owned = (
        self_project,
        self_output,
        cross_query,
        cross_memory,
        cross_output,
        feed_in,
        feed_out,
        bias_rows,
        feed_bias,
        norm_gains,
        norm_shifts,
    )
    micro_count = dec_lengths.shape[0]
    outputs = []
    grad_inputs = []
    grad_memories = []
    totals = None
    for batch_index in range(micro_count):
        hidden = hidden_in[batch_index * DEC : (batch_index + 1) * DEC]
        cot_rows = cotangent[batch_index * DEC : (batch_index + 1) * DEC]
        mem_rows = memory[batch_index * MEM : (batch_index + 1) * MEM]
        dec_len = dec_lengths[batch_index]
        mem_len = mem_lengths[batch_index]
        weights = fetch_forward(owned)
        saved, block_out = run_forward(weights, hidden, mem_rows, dec_len, mem_len)
        weights = fetch_backward(owned)
        grads, grad_hidden, grad_mem_rows = run_backward(
            weights, saved, hidden, mem_rows, cot_rows, dec_len, mem_len
        )
        grads = share_each(grads)
        if totals is None:
            totals = grads
        else:
            totals = tuple((earlier + later for earlier, later in zip(totals, grads)))
        outputs.append(block_out)
        grad_inputs.append(grad_hidden)
        grad_memories.append(grad_mem_rows)
    token_count = hidden_in.shape[0] * lax.axis_size(("dp", "shard"))
    factor = float(token_count) ** (-0.5)
    totals = tuple((item * factor for item in totals))
    return (
        jnp.concatenate(outputs, 0),
        jnp.concatenate(grad_inputs, 0),
        jnp.concatenate(grad_memories, 0),
        totals[0],
        totals[1],
        totals[2],
        totals[3],
        totals[4],
        totals[5],
        totals[6],
        totals[7],
        totals[8],
        totals[9],
        totals[10],
    )


def solution(mesh):
    in_specs = (
        P(("dp", "shard"), None),
        P(("dp", "shard"), None),
        P(("dp", "shard")),
        P(("dp", "shard")),
        P(("dp", "shard"), None),
        P(("dp", "shard"), None),
        P(("dp", "shard"), None),
        P(("dp", "shard"), None),
        P(("dp", "shard"), None),
        P(("dp", "shard"), None),
        P(("dp", "shard"), None),
        P(("dp", "shard"), None),
        P(None, ("dp", "shard")),
        P(("dp", "shard")),
        P(None, ("dp", "shard")),
        P(None, ("dp", "shard")),
    )
    out_specs = (
        P(("dp", "shard"), None),
        P(("dp", "shard"), None),
        P(("dp", "shard"), None),
        P(("dp", "shard"), None),
        P(("dp", "shard"), None),
        P(("dp", "shard"), None),
        P(("dp", "shard"), None),
        P(("dp", "shard"), None),
        P(("dp", "shard"), None),
        P(("dp", "shard"), None),
        P(None, ("dp", "shard")),
        P(("dp", "shard")),
        P(None, ("dp", "shard")),
        P(None, ("dp", "shard")),
    )
    return jax.shard_map(body, mesh=mesh, in_specs=in_specs, out_specs=out_specs, check_vma=False)
```

profile of v0, /device:TPU:0, one launch (start us, length us, event | category | flops | bytes accessed | tf_op | source)
XLA Modules:
  0.0 2093.2 jit_solution(9635032809920878126)
XLA Ops:
  11.9 43.7 %all-gather = bf16[32,32,7]{1,2,0:T(8,128)(2,1)S(1)} all-gather(bf16[1,32,7]{1,2,0:T(8,128)(2,1)} %bitcast.334), channel_id=1, replica_groups=mesh['dp'=8,'shard'=4] {'dp','shard'}, dimensions={0}, use_global_device_ids=true | all-gather | bytes 14784 | tf_op jit(solution)/shard_map/all_gather | solution.py:307
  55.8 37.0 %all-gather.1 = bf16[32,32,3]{1,2,0:T(4,128)(2,1)S(1)} all-gather(bf16[1,32,3]{1,2,0:T(4,128)(2,1)} %bitcast.335), channel_id=1, replica_groups=mesh['dp'=8,'shard'=4] {'dp','shard'}, dimensions={0}, use_global_device_ids=true | all-gather | bytes 6336 | tf_op jit(solution)/shard_map/all_gather | solution.py:309
  92.9 38.4 %all-gather.2 = bf16[32,32,3]{1,2,0:T(4,128)(2,1)S(1)} all-gather(bf16[1,32,3]{1,2,0:T(4,128)(2,1)} %bitcast.336), channel_id=1, replica_groups=mesh['dp'=8,'shard'=4] {'dp','shard'}, dimensions={0}, use_global_device_ids=true | all-gather | bytes 6336 | tf_op jit(solution)/shard_map/all_gather | solution.py:310
  131.4 36.7 %all-gather.3 = bf16[32,1,128]{2,1,0:T(2,128)(2,1)S(1)} all-gather(bf16[1,1,128]{2,1,0:T(2,128)(2,1)} %bitcast.337), channel_id=1, replica_groups=mesh['dp'=8,'shard'=4] {'dp','shard'}, dimensions={0}, use_global_device_ids=true | all-gather | bytes 8448 | tf_op jit(solution)/shard_map/all_gather | solution.py:308
  173.6 3.6 fusion.124
  179.8 3.6 fusion.127
  186.8 3.9 fusion.138
  195.0 9.7 all-gather.14.cloned.1.call-done
  211.4 51.3 %all-gather.18.cloned.1.call-done = bf16[1024,1024]{1,0:T(8,128)(2,1)} async-done(((bf16[32,1024]{1,0:T(8,128)(2,1)}), bf16[1024,1024]{1,0:T(8,128)(2,1)}) %all-gather.18.cloned.1.call-update) | async-done | bytes 2097168 | tf_op jit(solution)/shard_map/all_gather | solution.py:302
  275.6 45.0 %all-gather.20.cloned.1.call-done = bf16[1024,1024]{1,0:T(8,128)(2,1)} async-done(((bf16[32,1024]{1,0:T(8,128)(2,1)}), bf16[1024,1024]{1,0:T(8,128)(2,1)}) %all-gather.20.cloned.1.call-update) | async-done | bytes 2097168 | tf_op jit(solution)/shard_map/all_gather | solution.py:304
  328.9 70.9 %all-gather.22.cloned.1.call-done = bf16[1024,4096]{1,0:T(8,128)(2,1)} async-done(((bf16[32,4096]{1,0:T(8,128)(2,1)}), bf16[1024,4096]{1,0:T(8,128)(2,1)}) %all-gather.22.cloned.1.call-update) | async-done | bytes 8388624 | tf_op jit(solution)/shard_map/all_gather | solution.py:305
  399.8 6.0 convolution_add_fusion.3
  405.9 73.0 %all-gather.24.cloned.1.call-done = bf16[4096,1024]{1,0:T(8,128)(2,1)} async-done(((bf16[128,1024]{1,0:T(8,128)(2,1)}), bf16[4096,1024]{1,0:T(8,128)(2,1)}) %all-gather.24.cloned.1.call-update) | async-done | bytes 8388624 | tf_op jit(solution)/shard_map/all_gather | solution.py:306
  478.9 5.8 fusion.199
  492.2 8.1 convert_reduce_fusion.1
  500.2 3.1 multiply_reduce_fusion.8
  503.3 7.6 convert_reduce_fusion
  510.9 3.7 convert_reduce_fusion.11
  519.0 3.1 fusion.210
  523.5 16.9 convert_reduce_fusion.6
  540.4 3.3 convolution_convert_fusion.13
  545.5 2.9 fusion.208
  548.4 16.5 convert_reduce_fusion.12
  564.9 3.0 multiply_reduce_fusion.9
  592.3 4.2 convert_reduce_fusion.9
  598.5 3.0 convert_reduce_fusion.15
  604.1 5.2 convolution_add_fusion.4
  618.8 14.6 fusion.47
  633.4 15.8 fusion.44
  650.5 4.5 add_bitcast_fusion.1
  655.0 9.2 copy.169
  672.0 6.4 add_bitcast_fusion
  678.3 12.6 copy.167
  694.5 8.1 convolution_add_fusion.1
  703.0 4.2 fusion.174
  707.2 8.2 convolution_add_fusion
  716.1 39.4 %all-reduce = f32[4096]{0:T(1024)S(1)} all-reduce(f32[4096]{0:T(1024)S(1)} %add.487), channel_id=21, replica_groups=mesh['dp'=8,'shard'=4] {'dp','shard'}, use_global_device_ids=true, to_apply=%region_67.68.clone | all-reduce | flops 4096 | bytes 32768
  756.2 5.1 fusion.62
  761.4 5.2 fusion.63
  772.9 84.2 %reduce-scatter.37.cloned.1.call-done = f32[32,3]{1,0:T(8,128)} async-done(((f32[1024,3]{1,0:T(8,128)}), f32[32,3]{1,0:T(8,128)}) %reduce-scatter.37.cloned.1.call-update) | async-done | bytes 400
  859.0 129.8 %reduce-scatter.35.cloned.1.call-done = f32[32,7]{1,0:T(8,128)} async-done(((f32[1024,7]{1,0:T(8,128)}), f32[32,7]{1,0:T(8,128)}) %reduce-scatter.35.cloned.1.call-update) | async-done | bytes 912
  990.2 138.3 %reduce-scatter.25.cloned.1.call-done = f32[32,1024]{1,0:T(8,128)} async-done(((f32[1024,1024]{1,0:T(8,128)}), f32[32,1024]{1,0:T(8,128)}) %reduce-scatter.25.cloned.1.call-update) | async-done | bytes 131088 | tf_op jit(solution)/shard_map/reduce_scatter | solution.py:336
  1130.1 138.0 %reduce-scatter.23.cloned.1.call-done = f32[32,1024]{1,0:T(8,128)} async-done(((f32[1024,1024]{1,0:T(8,128)}), f32[32,1024]{1,0:T(8,128)}) %reduce-scatter.23.cloned.1.call-update) | async-done | bytes 131088 | tf_op jit(solution)/shard_map/reduce_scatter | solution.py:334
  1269.7 138.2 %reduce-scatter.21.cloned.1.call-done = f32[32,1024]{1,0:T(8,128)} async-done(((f32[1024,1024]{1,0:T(8,128)}), f32[32,1024]{1,0:T(8,128)}) %reduce-scatter.21.cloned.1.call-update) | async-done | bytes 131088 | tf_op jit(solution)/shard_map/reduce_scatter | solution.py:333
  1409.4 145.7 %reduce-scatter.33.cloned.1.call-done = f32[32,2048]{1,0:T(8,128)} async-done(((f32[1024,2048]{1,0:T(8,128)}), f32[32,2048]{1,0:T(8,128)}) %reduce-scatter.33.cloned.1.call-update) | async-done | bytes 262160
  1557.5 155.8 %reduce-scatter.31.cloned.1.call-done = f32[32,3072]{1,0:T(8,128)} async-done(((f32[1024,3072]{1,0:T(8,128)}), f32[32,3072]{1,0:T(8,128)}) %reduce-scatter.31.cloned.1.call-update) | async-done | bytes 393232
  1716.1 181.5 %reduce-scatter.27.cloned.1.call-done = f32[32,4096]{1,0:T(8,128)} async-done(((f32[1024,4096]{1,0:T(8,128)}), f32[32,4096]{1,0:T(8,128)}) %reduce-scatter.27.cloned.1.call-update) | async-done | bytes 524304 | tf_op jit(solution)/shard_map/reduce_scatter | solution.py:337
  1899.5 184.8 %reduce-scatter.29.cloned.1.call-done = f32[128,1024]{1,0:T(8,128)} async-done(((f32[4096,1024]{1,0:T(8,128)}), f32[128,1024]{1,0:T(8,128)}) %reduce-scatter.29.cloned.1.call-update) | async-done | bytes 524304 | tf_op jit(solution)/shard_map/reduce_scatter | solution.py:338
  (403 shorter events, 138.7 us)
Async XLA Ops:
  7.2 166.5 %all-gather.16.cloned.1.call-start = ((), (), s32[]{:S(2)}) async-start(), calls=%async_computation.12 | async-start | bytes 4325376 | tf_op jit(solution)/shard_map/all_gather | solution.py:303
  7.9 178.9 %all-gather.12.cloned.1.call-start = ((), (), s32[]{:S(2)}) async-start(), calls=%async_computation.10 | async-start | bytes 6488064 | tf_op jit(solution)/shard_map/all_gather | solution.py:300
  8.7 196.0 %all-gather.14.cloned.1.call-start = ((), (), s32[]{:S(2)}) async-start(), calls=%async_computation.11 | async-start | bytes 2162688 | tf_op jit(solution)/shard_map/all_gather | solution.py:301
  9.4 253.3 %all-gather.18.cloned.1.call-start = ((), (), s32[]{:S(2)}) async-start(), calls=%async_computation.13 | async-start | bytes 2162688 | tf_op jit(solution)/shard_map/all_gather | solution.py:302
  10.0 310.7 %all-gather.20.cloned.1.call-start = ((), (), s32[]{:S(2)}) async-start(), calls=%async_computation.14 | async-start | bytes 2162688 | tf_op jit(solution)/shard_map/all_gather | solution.py:304
  10.6 389.3 %all-gather.22.cloned.1.call-start = ((), (), s32[]{:S(2)}) async-start(), calls=%async_computation.15 | async-start | bytes 8650752 | tf_op jit(solution)/shard_map/all_gather | solution.py:305
  11.1 467.7 %all-gather.24.cloned.1.call-start = ((), (), s32[]{:S(2)}) async-start(), calls=%async_computation.16 | async-start | bytes 8650752 | tf_op jit(solution)/shard_map/all_gather | solution.py:306
  11.9 760.2 %reduce-scatter.39.cloned.1.call-start = ((), (), s32[]{:S(2)}) async-start(), calls=%async_computation.26 | async-start | bytes 540672
  193.7 13.3 copy-start.73
  193.9 13.1 copy-start.77
  194.1 13.5 copy-start.47
  195.0 12.4 copy-start.48
  211.4 109.3 %copy-start.42 = (bf16[128,1024]{1,0:T(8,128)(2,1)}, bf16[128,1024]{1,0:T(8,128)(2,1)S(1)}, u32[]{:S(2)}) copy-start(bf16[128,1024]{1,0:T(8,128)(2,1)S(1)} %get-tuple-element.136) | copy-start | bytes 786436
  478.9 6.0 slice-start
  478.9 6.5 slice-start.1
  488.2 15.1 copy-start.11
  492.2 8.1 copy-start.30
  492.2 18.8 copy-start.28
  492.2 8.1 copy-start.21
  503.3 7.6 copy-start.19
  572.2 7.0 copy-start.8
  592.3 264.8 %reduce-scatter.37.cloned.1.call-start = ((), (), s32[]{:S(2)}) async-start(), calls=%async_computation.25 | async-start | bytes 540672
  596.5 5.2 copy-start.95
  598.3 390.5 %reduce-scatter.35.cloned.1.call-start = ((), (), s32[]{:S(2)}) async-start(), calls=%async_computation.24 | async-start | bytes 540672
  604.1 524.4 %reduce-scatter.25.cloned.1.call-start = ((), (), s32[]{:S(2)}) async-start(), calls=%async_computation.19 | async-start | bytes 4325376 | tf_op jit(solution)/shard_map/reduce_scatter | solution.py:336
  609.3 658.8 %reduce-scatter.23.cloned.1.call-start = ((), (), s32[]{:S(2)}) async-start(), calls=%async_computation.18 | async-start | bytes 4325376 | tf_op jit(solution)/shard_map/reduce_scatter | solution.py:334
  614.0 793.8 %reduce-scatter.21.cloned.1.call-start = ((), (), s32[]{:S(2)}) async-start(), calls=%async_computation.17 | async-start | bytes 4325376 | tf_op jit(solution)/shard_map/reduce_scatter | solution.py:333
  618.8 936.3 %reduce-scatter.33.cloned.1.call-start = ((), (), s32[]{:S(2)}) async-start(), calls=%async_computation.23 | async-start | bytes 8650752
  633.4 15.8 copy-start.58
  633.4 15.8 copy-start.68
  633.4 15.8 copy-start.80
  664.2 5.9 copy-start.27
  664.2 5.9 copy-start.65
  664.2 5.9 copy-start.86
  664.2 1049.1 %reduce-scatter.31.cloned.1.call-start = ((), (), s32[]{:S(2)}) async-start(), calls=%async_computation.22 | async-start | bytes 12976128
  690.9 1206.6 %reduce-scatter.27.cloned.1.call-start = ((), (), s32[]{:S(2)}) async-start(), calls=%async_computation.20 | async-start | bytes 17301504 | tf_op jit(solution)/shard_map/reduce_scatter | solution.py:337
  702.7 1381.6 %reduce-scatter.29.cloned.1.call-start = ((), (), s32[]{:S(2)}) async-start(), calls=%async_computation.21 | async-start | bytes 17301504 | tf_op jit(solution)/shard_map/reduce_scatter | solution.py:338
  715.4 40.7 %copy-start.32 = (f32[128,1024]{1,0:T(8,128)S(1)}, f32[128,1024]{1,0:T(8,128)}, u32[]{:S(2)}) copy-start(f32[128,1024]{1,0:T(8,128)} %get-tuple-element.108) | copy-start | bytes 1572868
  715.4 40.7 %copy-start.66 = (bf16[16,64,128]{2,1,0:T(8,128)(2,1)S(1)}, bf16[16,64,128]{2,1,0:T(8,128)(2,1)}, u32[]{:S(2)}) copy-start(bf16[16,64,128]{2,1,0:T(8,128)(2,1)} %get-tuple-element.178) | copy-start | bytes 786436
  715.4 40.7 %copy-start.87 = (bf16[16,64,128]{2,1,0:T(8,128)(2,1)S(1)}, bf16[16,64,128]{2,1,0:T(8,128)(2,1)}, u32[]{:S(2)}) copy-start(bf16[16,64,128]{2,1,0:T(8,128)(2,1)} %get-tuple-element.176) | copy-start | bytes 786436
  715.4 40.7 %copy-start.91 = (bf16[16,64,128]{2,1,0:T(8,128)(2,1)S(1)}, bf16[16,64,128]{2,1,0:T(8,128)(2,1)}, u32[]{:S(2)}) copy-start(bf16[16,64,128]{2,1,0:T(8,128)(2,1)} %copy-done.90) | copy-start | bytes 786436
  756.1 5.2 copy-start.35
  756.1 5.2 copy-start.64
  756.2 5.2 copy-start.85
  756.2 5.2 copy-start.89
  761.3 6.1 copy-start.78
  761.3 6.1 copy-start.79
  761.3 6.9 copy-start.97
  (71 other events, 178.4 us)
Sparse Core Ops, SparseCore 0:
  10.9 64.7 all-gather.15
  78.5 68.2 all-gather.11
  149.7 54.8 all-gather.13
  207.4 55.2 all-gather.17
  265.4 55.2 all-gather.19
  323.4 76.3 all-gather.21
  402.7 76.1 all-gather.23
  592.4 132.6 reduce-scatter.38
  727.4 129.6 reduce-scatter.36
  859.2 129.5 reduce-scatter.34
  991.2 137.2 reduce-scatter.24
  1130.7 137.3 reduce-scatter.22
  1270.5 137.3 reduce-scatter.20
  1410.1 144.9 reduce-scatter.32
  1562.0 151.2 reduce-scatter.30
  1715.4 182.0 reduce-scatter.26
  1899.7 184.5 reduce-scatter.28
where the time goes:
time: 2110 us; the launch traced here: 2090 us
  waiting for transfers between devices  1550 us (73%)
  matrix products  239 us (11%)
  blocking collectives  195 us (9%)
  local copies, waits for them, and re-layouts  65.7 us (3%)
  other arithmetic  25 us (1%)
    unnamed x22, waiting for transfers between devices  520 us
    reduce_scatter x1, waiting for transfers between devices, share_each(): lax.psum_scatter(grads[6], ('dp', 'shard'), scatter_dimension=0, tiled=True)  185 us
    reduce_scatter x1, waiting for transfers between devices, share_each(): lax.psum_scatter(grads[5], ('dp', 'shard'), scatter_dimension=0, tiled=True)  181 us
    reduce_scatter x1, waiting for transfers between devices, share_each(): lax.psum_scatter(grads[4], ('dp', 'shard'), scatter_dimension=0, tiled=True)  138 us
    reduce_scatter x1, waiting for transfers between devices, share_each(): lax.psum_scatter(grads[1], ('dp', 'shard'), scatter_dimension=0, tiled=True)  138 us
    reduce_scatter x1, waiting for transfers between devices, share_each(): lax.psum_scatter(grads[2], ('dp', 'shard'), scatter_dimension=0, tiled=True)  138 us
    all_gather x1, waiting for transfers between devices, fetch_forward(): lax.all_gather(owned[6], ('dp', 'shard'), axis=0, tiled=True)  73 us
    all_gather x1, waiting for transfers between devices, fetch_forward(): lax.all_gather(owned[5], ('dp', 'shard'), axis=0, tiled=True)  70.9 us
  transfers between devices with their start and end apart: 17, of which 14 were waited for; matrix products, arithmetic and copies ran while one was open for 10% of the time, Pallas kernels for 0%

commit v1 on v0

v1 whole, which is shorter than its diff:
```python
import functools
import math

import jax
import jax.numpy as jnp
from jax import lax
from jax.experimental import pallas as pl
from jax.experimental.pallas import tpu as pltpu
from jax.sharding import PartitionSpec as P

D = 1024
HEADS = 16
HEAD_DIM = 64
DEC = 128
MEM = 256
AXES = ("dp", "shard")
MESH_ID = pl.DeviceIdType.MESH
BF16 = jnp.bfloat16
F32 = jnp.float32

alpha_res = 300.0**0.25
epsilon = 1e-05
gelu_coef = math.sqrt(2.0 / math.pi)

SIZES = {"z": 4, "x": 2, "y": 2}
SLOT = {"x": 0, "y": 1, "s": 2, "z": 2}


def my_place():
    dp, shard = lax.axis_index("dp"), lax.axis_index("shard")
    return {
        "z": lax.div(dp, 2),
        "x": lax.rem(dp, 2),
        "y": lax.div(shard, 2),
        "c": lax.rem(shard, 2),
    }


def device_of(place):
    return (place["z"] * 2 + place["x"], place["y"] * 2 + place["c"])


def partners(place, dim):
    if dim == "z":
        return [(2 + o, dict(place, z=lax.rem(place["z"] + o, 4))) for o in (1, 2, 3)]
    key = "c" if dim == "s" else dim
    return [(SLOT[dim], dict(place, **{key: 1 - place[key]}))]


def greet(place):
    barrier = pltpu.get_barrier_semaphore()
    others = [p for dim in "xysz" for _, p in partners(place, dim)]
    for other in others:
        pl.semaphore_signal(barrier, inc=1, device_id=device_of(other), device_id_type=MESH_ID)
    pl.semaphore_wait(barrier, len(others))


def block_at(place, whole):
    return tuple(pl.ds(0, SIZES.get(d, 2)) if d in whole else place[d] for d in ("z", "x", "y", "c"))


class Gather:
    def __init__(self, place, own, full, start, width, order, number, send_sem, recv_sem):
        self.place, self.own, self.full, self.order, self.number = place, own, full, order, number
        self.columns = pl.ds(start, width)
        self.send_sem, self.recv_sem = send_sem, recv_sem
        self.sent = []
        self.waiting = []

    def send(self, source, index, dim):
        target = self.full.at[(*index, slice(None), self.columns)]
        self.waiting = []
        for slot, other in partners(self.place, dim):
            copy = pltpu.make_async_remote_copy(
                src_ref=source,
                dst_ref=target,
                send_sem=self.send_sem.at[self.number, slot],
                recv_sem=self.recv_sem.at[self.number, slot],
                device_id=device_of(other),
                device_id_type=MESH_ID,
            )
            copy.start()
            self.waiting.append(copy)
            self.sent.append(copy)

    def arrive(self):
        for copy in self.waiting:
            copy.wait_recv()

    def stage(self, number):
        if number > 0:
            self.arrive()
        if number == 0:
            self.send(self.own.at[:, self.columns], block_at(self.place, ""), self.order[0])
        elif number < 3:
            index = block_at(self.place, self.order[:number])
            self.send(self.full.at[(*index, slice(None), self.columns)], index, self.order[number])
        elif number == 3:
            index = block_at(self.place, "zxy")
            self.send(self.full.at[(*index, slice(None), self.columns)], index, "s")

    def drain(self):
        for copy in self.sent:
            copy.wait_send()


def schedule(count, stages, lag):
    for step in range(count + (stages - 1) * lag):
        for stage in reversed(range(stages)):
            if 0 <= step - stage * lag < count:
                yield step - stage * lag, stage


def gather_plan(blocks, size):
    plan = []
    for unit, (rows, columns) in enumerate(blocks):
        width = min(columns, size // rows)
        for start in range(0, columns, width):
            plan.append((unit, start, width, GATHER_ORDERS[len(plan) % len(GATHER_ORDERS)]))
    return plan


LAG = 3
WIDTH = 512
SLOTS = 3
GATHER_ORDERS = ("xzy", "zyx", "zxy", "yzx", "zyx", "zxy")


def gather_kernel(plan, units, *refs):
    own, full = refs[:units], refs[units : 2 * units]
    send_sem, recv_sem, own_sem = refs[2 * units :]
    place = my_place()
    greet(place)
    here = []
    for unit in range(units):
        copy = pltpu.make_async_copy(own[unit], full[unit].at[block_at(place, "")], own_sem.at[unit])
        copy.start()
        here.append(copy)
    chunks = [
        Gather(place, own[unit], full[unit], start, width, order, number, send_sem, recv_sem)
        for number, (unit, start, width, order) in enumerate(plan)
    ]
    for copy in here:
        copy.wait()
    for number, stage in schedule(len(chunks), 5, LAG):
        chunks[number].stage(stage)
    for chunk in chunks:
        chunk.drain()


def gather_all(owned):
    units = len(owned)
    plan = gather_plan([a.shape for a in owned], 32 * WIDTH)
    any_spec = pl.BlockSpec(memory_space=pl.ANY)
    return pl.pallas_call(
        functools.partial(gather_kernel, plan, units),
        out_shape=[jax.ShapeDtypeStruct((4, 2, 2, 2, *a.shape), a.dtype) for a in owned],
        in_specs=[any_spec] * units,
        out_specs=[any_spec] * units,
        scratch_shapes=[
            pltpu.SemaphoreType.DMA((len(plan), 6)),
            pltpu.SemaphoreType.DMA((len(plan), 6)),
            pltpu.SemaphoreType.DMA((units,)),
        ],
        compiler_params=pltpu.CompilerParams(collective_id=0, has_side_effects=True),
        name="gather_parameters",
    )(*owned)


SCATTER_ORDERS = ("yzx", "xyz", "yxz", "xzy", "xyz", "yxz")


def rings_of(order):
    keys = [("s", "zxy")]
    left = "zxy"
    for dim in order:
        left = left.replace(dim, "")
        keys.append((dim, left))
    return keys


def ring_shape(key, width):
    dim, left = key
    return (SLOTS, 3 if dim == "z" else 1, *[SIZES[d] for d in left], 32, width)


class Rings:
    def __init__(self, place, keys, buffers, credit, plan):
        self.place, self.credit = place, credit
        self.number = {key: k for k, key in enumerate(keys)}
        self.buffer = dict(zip(keys, buffers))
        self.uses = {key: 0 for key in keys}
        for _, _, _, _, _, order in plan:
            for key in rings_of(order):
                self.uses[key] += 1
        self.turn = {key: 0 for key in keys}

    def take(self, key):
        turn = self.turn[key]
        self.turn[key] += 1
        if turn >= SLOTS:
            for slot, _ in partners(self.place, key[0]):
                pl.semaphore_wait(self.credit.at[self.number[key], slot], 1)
        return turn

    def give(self, key, turn):
        if turn + SLOTS >= self.uses[key]:
            return
        for slot, other in partners(self.place, key[0]):
            if key[0] == "z":
                other = dict(self.place, z=lax.rem(self.place["z"] + 6 - slot, 4))
            pl.semaphore_signal(
                self.credit.at[self.number[key], slot], inc=1, device_id=device_of(other), device_id_type=MESH_ID
            )


class Scatter:
    def __init__(self, place, rings, grads, out, scale, piece, number, send_sem, recv_sem):
        _, row, rows, start, width, self.order = piece
        self.place, self.rings, self.grads, self.out, self.scale, self.number = place, rings, grads, out, scale, number
        self.part = (pl.ds(row, rows), pl.ds(start, width))
        self.corner = (pl.ds(0, rows), pl.ds(0, width))
        self.keys = rings_of(self.order)
        self.send_sem, self.recv_sem = send_sem, recv_sem
        self.sent = []

    def send(self, stage):
        key = self.keys[stage]
        dim, left = key
        self.turn = self.rings.take(key)
        buffer = self.rings.buffer[key]
        self.waiting = []
        for k, (slot, other) in enumerate(partners(self.place, dim)):
            copy = pltpu.make_async_remote_copy(
                src_ref=self.grads.at[(*block_at(other, left), *self.part)],
                dst_ref=buffer.at[(self.turn % SLOTS, k, *[slice(None)] * len(left), *self.corner)],
                send_sem=self.send_sem.at[self.number, slot],
                recv_sem=self.recv_sem.at[self.number, slot],
                device_id=device_of(other),
                device_id_type=MESH_ID,
            )
            copy.start()
            self.waiting.append(copy)
            self.sent.append(copy)

    def add(self, stage):
        key = self.keys[stage]
        dim, left = key
        for copy in self.waiting:
            copy.wait_recv()
        buffer = self.rings.buffer[key]
        slot = self.turn % SLOTS

        def total(inner, own):
            value = self.grads[(*own, *self.part)].astype(F32)
            for k in range(3 if dim == "z" else 1):
                value += buffer[(slot, k, *inner, *self.corner)].astype(F32)
            return value

        own = block_at(self.place, left)
        if not left:
            self.out[self.part] = total((), own) * self.scale
        elif len(left) == 1:
            inner = (slice(None),)
            self.grads[(*own, *self.part)] = total(inner, own).astype(BF16)
        else:
            first = left[0]

            def body(i, _):
                here = dict(self.place, **{first: i})
                index = block_at(here, left[1:])
                inner = (i, *[slice(None)] * (len(left) - 1))
                self.grads[(*index, *self.part)] = total(inner, index).astype(BF16)
                return 0

            lax.fori_loop(0, SIZES[first], body, 0)
        self.rings.give(key, self.turn)

    def stage(self, number):
        if number > 0:
            self.add(number - 1)
        if number < 4:
            self.send(number)

    def drain(self):
        for copy in self.sent:
            copy.wait_send()


def scatter_plan(blocks, width):
    plan = []
    for unit, (rows, columns) in enumerate(blocks):
        for row in range(0, rows, 32):
            for start in range(0, columns, width):
                order = SCATTER_ORDERS[len(plan) % len(SCATTER_ORDERS)]
                plan.append((unit, row, min(rows, 32), start, min(columns, width), order))
    return plan


def ring_keys():
    return sorted({key for order in SCATTER_ORDERS for key in rings_of(order)})


def scatter_kernel(plan, scale, units, *refs):
    grads, outs, held = refs[:units], refs[units : 2 * units], refs[2 * units : 3 * units]
    keys = ring_keys()
    buffers = refs[3 * units : 3 * units + len(keys)]
    send_sem, recv_sem, load_sem, credit = refs[3 * units + len(keys) :]
    place = my_place()
    greet(place)
    rings = Rings(place, keys, buffers, credit, plan)
    loads, chunks = [], []
    everywhere = (slice(None),) * 4
    for number, piece in enumerate(plan):
        unit = piece[0]
        chunk = Scatter(place, rings, held[unit], outs[unit], scale, piece, number, send_sem, recv_sem)
        where = (*everywhere, *chunk.part)
        load = pltpu.make_async_copy(grads[unit].at[where], held[unit].at[where], load_sem.at[number])
        load.start()
        loads.append(load)
        chunks.append(chunk)

    for number, stage in schedule(len(chunks), 5, LAG):
        if stage == 0:
            loads[number].wait()
        chunks[number].stage(stage)
    for chunk in chunks:
        chunk.drain()


def scatter_all(grads, scale):
    units = len(grads)
    plan = scatter_plan([a.shape[4:] for a in grads], WIDTH)
    any_spec = pl.BlockSpec(memory_space=pl.ANY)
    vmem = pl.BlockSpec(memory_space=pltpu.VMEM)
    keys = ring_keys()
    return pl.pallas_call(
        functools.partial(scatter_kernel, plan, scale, units),
        out_shape=[jax.ShapeDtypeStruct(a.shape[4:], F32) for a in grads],
        in_specs=[any_spec] * units,
        out_specs=[vmem] * units,
        scratch_shapes=[pltpu.VMEM(a.shape, BF16) for a in grads]
        + [pltpu.VMEM(ring_shape(key, WIDTH), BF16) for key in keys]
        + [
            pltpu.SemaphoreType.DMA((len(plan), 6)),
            pltpu.SemaphoreType.DMA((len(plan), 6)),
            pltpu.SemaphoreType.DMA((len(plan),)),
            pltpu.SemaphoreType.REGULAR((len(keys), 6)),
        ],
        compiler_params=pltpu.CompilerParams(collective_id=1, has_side_effects=True, vmem_limit_bytes=58 * 2**20),
        name="scatter_gradients",
    )(*grads)


def gelu_tanh(value):
    inner = gelu_coef * (value + 0.044715 * value * value * value)
    return 0.5 * value * (1.0 + jnp.tanh(inner))


def gelu_slope(value):
    inner = gelu_coef * (value + 0.044715 * value * value * value)
    tangent = jnp.tanh(inner)
    return 0.5 * (1.0 + tangent) + 0.5 * value * (1.0 - tangent * tangent) * gelu_coef * (
        1.0 + 3.0 * 0.044715 * value * value
    )


def product(rows_mat, weight):
    return jnp.dot(rows_mat, weight, preferred_element_type=F32)


def times_trans(rows_mat, weight):
    return jnp.einsum("tj,ij->ti", rows_mat, weight, preferred_element_type=F32)


def outer_sum(left_rows, right_rows):
    return jnp.einsum("ti,tj->ij", left_rows, right_rows, preferred_element_type=F32)


def column_total(rows_mat):
    return jnp.sum(rows_mat.astype(F32), 0)


def layer_norm(resid, gain, shift):
    center = resid - jnp.mean(resid, -1, keepdims=True)
    inv_dev = lax.rsqrt(jnp.mean(center * center, -1, keepdims=True) + epsilon)
    scaled = center * inv_dev
    return (scaled * gain + shift, scaled, inv_dev)


def norm_back(grad_out, scaled, inv_dev, gain):
    grad_scaled = grad_out * gain
    grad_resid = inv_dev * (
        grad_scaled
        - jnp.mean(grad_scaled, -1, keepdims=True)
        - scaled * jnp.mean(grad_scaled * scaled, -1, keepdims=True)
    )
    return (grad_resid, jnp.sum(grad_out * scaled, 0), jnp.sum(grad_out, 0))


def split_heads(matrix, length):
    return matrix.reshape(-1, length, HEADS, HEAD_DIM)


def merge_heads(tensor):
    return tensor.reshape(-1, D)


def scores_of(query_rows, key_rows, allowed):
    keys = allowed.shape[-1]
    raw = jnp.einsum(
        "sqhe,skhe->shqk",
        split_heads(query_rows, DEC),
        split_heads(key_rows, keys),
        preferred_element_type=F32,
    )
    return jnp.where(allowed[:, None], raw * HEAD_DIM ** (-0.5), -1000000000.0)


def attend(query_rows, key_rows, value_rows, allowed):
    scores = scores_of(query_rows, key_rows, allowed)
    top_score = jnp.max(scores, -1, keepdims=True)
    log_total = top_score + jnp.log(jnp.sum(jnp.exp(scores - top_score), -1, keepdims=True))
    probabilities = jnp.exp(scores - log_total).astype(BF16)
    mixed = jnp.einsum(
        "shqk,skhe->sqhe",
        probabilities,
        split_heads(value_rows, allowed.shape[-1]),
        preferred_element_type=F32,
    )
    return (merge_heads(mixed).astype(BF16), log_total)


def attend_back(query_rows, key_rows, value_rows, allowed, log_total, grad_mixed):
    keys = allowed.shape[-1]
    probabilities = jnp.exp(scores_of(query_rows, key_rows, allowed) - log_total)
    grad_heads = split_heads(grad_mixed, DEC)
    grad_value = jnp.einsum(
        "shqk,sqhe->skhe", probabilities.astype(BF16), grad_heads, preferred_element_type=F32
    )
    grad_probs = jnp.einsum(
        "sqhe,skhe->shqk", grad_heads, split_heads(value_rows, keys), preferred_element_type=F32
    )
    grad_scores = probabilities * (
        grad_probs - jnp.sum(probabilities * grad_probs, -1, keepdims=True)
    )
    grad_raw = (grad_scores * HEAD_DIM ** (-0.5)).astype(BF16)
    grad_query = jnp.einsum(
        "shqk,skhe->sqhe", grad_raw, split_heads(key_rows, keys), preferred_element_type=F32
    )
    grad_key = jnp.einsum(
        "shqk,sqhe->skhe", grad_raw, split_heads(query_rows, DEC), preferred_element_type=F32
    )
    return (
        merge_heads(grad_query).astype(BF16),
        merge_heads(grad_key).astype(BF16),
        merge_heads(grad_value).astype(BF16),
    )


def masks_for(dec_lengths, mem_lengths):
    row_ids = jnp.arange(DEC)
    inside = row_ids[None, :] < dec_lengths[:, None]
    valid_rows = inside.reshape(-1, 1)
    causal = (row_ids[None, None, :] <= row_ids[None, :, None]) & inside[:, None, :]
    mem_seen = (jnp.arange(MEM)[None, :] < mem_lengths[:, None])[:, None, :]
    mem_seen = jnp.broadcast_to(mem_seen, (mem_lengths.shape[0], DEC, MEM))
    return (valid_rows, causal, mem_seen)


def run_forward(weights, hidden, mem_rows, dec_lengths, mem_lengths):
    (
        self_project,
        self_output,
        cross_query,
        cross_memory,
        cross_output,
        feed_in,
        feed_out,
        bias_rows,
        feed_bias,
        norm_gains,
        norm_shifts,
    ) = weights
    bias_full = bias_rows.astype(F32)
    gain_full = norm_gains.astype(F32)
    shift_full = norm_shifts.astype(F32)
    valid_rows, causal, mem_seen = masks_for(dec_lengths, mem_lengths)
    projected = product(hidden, self_project)
    query_rows = (projected[:, :D] + bias_full[0]).astype(BF16)
    key_rows = projected[:, D : 2 * D].astype(BF16)
    value_rows = (projected[:, 2 * D :] + bias_full[1]).astype(BF16)
    mixed, log_one = attend(query_rows, key_rows, value_rows, causal)
    resid_one = alpha_res * hidden.astype(F32) + product(mixed, self_output) + bias_full[2]
    first, scaled_one, inv_one = layer_norm(resid_one, gain_full[0], shift_full[0])
    first = first.astype(BF16)
    cross_q = (product(first, cross_query) + bias_full[3]).astype(BF16)
    mem_proj = product(mem_rows, cross_memory)
    cross_k = mem_proj[:, :D].astype(BF16)
    cross_v = (mem_proj[:, D:] + bias_full[4]).astype(BF16)
    mixed_two, log_two = attend(cross_q, cross_k, cross_v, mem_seen)
    resid_two = (
        alpha_res * first.astype(F32) + product(mixed_two, cross_output) + bias_full[5]
    )
    second, scaled_two, inv_two = layer_norm(resid_two, gain_full[1], shift_full[1])
    second = second.astype(BF16)
    pre_act = product(second, feed_in) + feed_bias.astype(F32)
    active = gelu_tanh(pre_act).astype(BF16)
    resid_three = alpha_res * second.astype(F32) + product(active, feed_out) + bias_full[6]
    normed, scaled_three, inv_three = layer_norm(resid_three, gain_full[2], shift_full[2])
    block_out = jnp.where(valid_rows, normed, 0.0).astype(BF16)
    saved = (
        query_rows,
        key_rows,
        value_rows,
        log_one,
        mixed,
        scaled_one,
        inv_one,
        first,
        cross_q,
        cross_k,
        cross_v,
        log_two,
        mixed_two,
        scaled_two,
        inv_two,
        second,
        pre_act,
        active,
        scaled_three,
        inv_three,
    )
    return (saved, block_out)


def run_backward(weights, saved, hidden, mem_rows, cot_rows, dec_lengths, mem_lengths):
    (
        self_project,
        self_output,
        cross_query,
        cross_memory,
        cross_output,
        feed_in,
        feed_out,
        bias_rows,
        feed_bias,
        norm_gains,
        norm_shifts,
    ) = weights
    (
        query_rows,
        key_rows,
        value_rows,
        log_one,
        mixed,
        scaled_one,
        inv_one,
        first,
        cross_q,
        cross_k,
        cross_v,
        log_two,
        mixed_two,
        scaled_two,
        inv_two,
        second,
        pre_act,
        active,
        scaled_three,
        inv_three,
    ) = saved
    gain_full = norm_gains.astype(F32)
    valid_rows, causal, mem_seen = masks_for(dec_lengths, mem_lengths)
    grad_top = jnp.where(valid_rows, cot_rows.astype(F32), 0.0)
    grad_three, gain_three, shift_three = norm_back(grad_top, scaled_three, inv_three, gain_full[2])
    branch_three = grad_three.astype(BF16)
    grad_feed_out = outer_sum(active, branch_three)
    grad_pre = (times_trans(branch_three, feed_out) * gelu_slope(pre_act)).astype(BF16)
    grad_feed_in = outer_sum(second, grad_pre)
    grad_second = (alpha_res * grad_three + times_trans(grad_pre, feed_in)).astype(BF16)
    grad_two, gain_two, shift_two = norm_back(
        grad_second.astype(F32), scaled_two, inv_two, gain_full[1]
    )
    branch_two = grad_two.astype(BF16)
    grad_cross_output = outer_sum(mixed_two, branch_two)
    grad_mixed_two = times_trans(branch_two, cross_output).astype(BF16)
    grad_cq, grad_ck, grad_cv = attend_back(
        cross_q, cross_k, cross_v, mem_seen, log_two, grad_mixed_two
    )
    grad_mem_proj = jnp.concatenate([grad_ck, grad_cv], 1)
    grad_cross_memory = outer_sum(mem_rows, grad_mem_proj)
    grad_mem_rows = times_trans(grad_mem_proj, cross_memory).astype(BF16)
    grad_cross_query = outer_sum(first, grad_cq)
    grad_first = (alpha_res * grad_two + times_trans(grad_cq, cross_query)).astype(BF16)
    grad_one, gain_one, shift_one = norm_back(
        grad_first.astype(F32), scaled_one, inv_one, gain_full[0]
    )
    branch_one = grad_one.astype(BF16)
    grad_self_output = outer_sum(mixed, branch_one)
    grad_mixed = times_trans(branch_one, self_output).astype(BF16)
    grad_q, grad_k, grad_v = attend_back(
        query_rows, key_rows, value_rows, causal, log_one, grad_mixed
    )
    grad_projected = jnp.concatenate([grad_q, grad_k, grad_v], 1)
    grad_self_project = outer_sum(hidden, grad_projected)
    grad_hidden = (alpha_res * grad_one + times_trans(grad_projected, self_project)).astype(
        BF16
    )
    grad_bias_rows = jnp.stack(
        [
            column_total(grad_q),
            column_total(grad_v),
            column_total(branch_one),
            column_total(grad_cq),
            column_total(grad_cv),
            column_total(branch_two),
            column_total(branch_three),
        ]
    )
    grads = (
        grad_self_project,
        grad_self_output,
        grad_cross_query,
        grad_cross_memory,
        grad_cross_output,
        grad_feed_in,
        grad_feed_out,
        grad_bias_rows,
        column_total(grad_pre),
        jnp.stack([gain_one, gain_two, gain_three]),
        jnp.stack([shift_one, shift_two, shift_three]),
    )
    return (grads, grad_hidden, grad_mem_rows)


SMALL = 13


def pack_small(bias_rows, feed_bias, norm_gains, norm_shifts):
    rows = jnp.concatenate([bias_rows, norm_gains, norm_shifts], 0)
    span = rows.shape[1]
    lane = lax.broadcasted_iota(jnp.int32, (SMALL, 128), 1) // span
    rows = jnp.where(lane == lax.axis_index("shard"), jnp.tile(rows, (1, 128 // span)), 0)
    rest = jnp.zeros((2, 128), BF16)
    return jnp.concatenate([rows, feed_bias[None], rest], 0)


def unpack_small(blocks):
    rows = blocks[:, :SMALL].reshape(-1, 4, SMALL, 128).astype(F32).sum(1).astype(BF16)
    rows = rows.transpose(1, 0, 2).reshape(SMALL, D)
    return rows[:7], blocks[:, SMALL].reshape(-1), rows[7:10], rows[10:]


def pack_small_grads(grad_bias_rows, grad_feed_bias, grad_gains, grad_shifts):
    rows = jnp.concatenate([grad_bias_rows, grad_gains, grad_shifts], 0)
    rows = rows.reshape(SMALL, 8, 1, 128).transpose(1, 2, 0, 3)
    rows = jnp.broadcast_to(rows, (8, 4, SMALL, 128)).reshape(32, SMALL, 128)
    feed = grad_feed_bias.reshape(32, 1, 128)
    return jnp.concatenate([rows, feed, jnp.zeros((32, 2, 128), F32)], 1).astype(BF16)


def unpack_small_grads(block):
    rows = lax.dynamic_slice_in_dim(block[:SMALL], lax.axis_index("shard") * 32, 32, 1)
    return rows[:7], block[SMALL], rows[7:10], rows[10:]


def gather_by_collectives(owned):
    axis = [0] * 7 + [1, 0, 1, 1]
    return tuple(lax.all_gather(a, AXES, axis=d, tiled=True) for a, d in zip(owned, axis))


def scatter_by_collectives(grads, factor):
    axis = [0] * 7 + [1, 0, 1, 1]
    return tuple(
        lax.psum_scatter(a * factor, AXES, scatter_dimension=d, tiled=True) for a, d in zip(grads, axis)
    )


def body(by_kernel, hidden_in, memory, dec_lengths, mem_lengths, cotangent, *owned):
    token_count = hidden_in.shape[0] * lax.axis_size(AXES)
    factor = float(token_count) ** (-0.5)
    if by_kernel:
        big = gather_all((pack_small(*owned[7:]), *owned[:7]))
        small = unpack_small(big[0].reshape(-1, 16, 128))
        weights = (*[a.reshape(-1, a.shape[-1]) for a in big[1:]], *small)
    else:
        weights = gather_by_collectives(owned)
    saved, block_out = run_forward(weights, hidden_in, memory, dec_lengths, mem_lengths)
    grads, grad_hidden, grad_memory = run_backward(
        weights, saved, hidden_in, memory, cotangent, dec_lengths, mem_lengths
    )
    if by_kernel:
        small = pack_small_grads(*grads[7:])
        packed = [a.astype(BF16).reshape(32, -1, a.shape[-1]) for a in grads[:7]]
        packed = [a.reshape(4, 2, 2, 2, *a.shape[1:]) for a in (small, *packed)]
        shares = scatter_all(packed, factor)
        totals = (*shares[1:], *unpack_small_grads(shares[0]))
    else:
        totals = scatter_by_collectives(grads, factor)
    return (block_out, grad_hidden, grad_memory, *totals)


def solution(mesh):
    rows, columns, vector = P(AXES, None), P(None, AXES), P(AXES)
    in_specs = (rows, rows, vector, vector, rows, *[rows] * 7, columns, vector, columns, columns)
    out_specs = (rows, rows, rows, *[rows] * 7, columns, vector, columns, columns)
    by_kernel = mesh.shape["dp"] == 8 and mesh.shape["shard"] == 4
    return jax.shard_map(
        functools.partial(body, by_kernel), mesh=mesh, in_specs=in_specs, out_specs=out_specs, check_vma=False
    )
```

time: 2110 us -> 569 us (0.27)
  waiting for transfers between devices: 1550 us -> 0 us
  Pallas kernels: 0 us -> 333 us
  blocking collectives: 195 us -> 0 us
  matrix products: 239 us -> 156 us
    reduce_scatter x5 -> x0, waiting for transfers between devices: 781 us -> none  [the longest x1 185 us: share_each(): lax.psum_scatter(grads[6], ('dp', 'shard'), scatter_dimension=0, tiled=True)]
    unnamed x22 -> x0, waiting for transfers between devices: 520 us -> none
    pallas_call x0 -> x2, Pallas kernels: none -> 333 us  [the longest x1 180 us: gather_all(): pl.pallas_call(functools.partial(gather_kernel, plan, units), out_shape=[...]
    all_gather x7 -> x0, waiting for transfers between devices: 250 us -> none  [the longest x1 73 us: fetch_forward(): lax.all_gather(owned[6], ('dp', 'shard'), axis=0, tiled=True)]
    all_gather x4 -> x0, blocking collectives: 156 us -> none  [the longest x1 43.7 us: fetch_forward(): lax.all_gather(owned[7], ('dp', 'shard'), axis=1, tiled=True)]
    dot_general x66 -> x33, matrix products: 239 us -> 156 us  [the longest x2 35.2 us: attend_back(): jnp.einsum('shqk,sqhe->skhe', grad_raw, split_heads(query_rows, DEC), pre...]
    unnamed x1 -> x0, blocking collectives: 39.4 us -> none
    unnamed x216 -> x110, local copies, waits for them, and re-layouts: 45.2 us -> 22.7 us
  transfers between devices with their start and end apart: 17 -> 0, of which waited for: 14 -> 0; matrix products, arithmetic and copies ran while one was open for 10% -> 0% of each run, Pallas kernels for 0% -> 0%
where the time goes in v1:
time: 569 us; the launch traced here: 563 us
  Pallas kernels  333 us (59%)
  matrix products  156 us (27%)
  local copies, waits for them, and re-layouts  60.7 us (11%)
  other arithmetic  11.2 us (2%)
    pallas_call x1, Pallas kernels, gather_all(): pl.pallas_call(functools.partial(gather_kernel, plan, units), out_shape=[...  180 us
    pallas_call x1, Pallas kernels, scatter_all(): pl.pallas_call(functools.partial(scatter_kernel, plan, scale, units), out...  153 us
    dot_general x2, matrix products, attend_back(): jnp.einsum('shqk,sqhe->skhe', grad_raw, split_heads(query_rows, DEC), pre...  35.2 us
    dot_general x2, matrix products, attend_back(): jnp.einsum('shqk,skhe->sqhe', grad_raw, split_heads(key_rows, keys), pref...  33.5 us
    dot_general x7, matrix products, outer_sum(): jnp.einsum('ti,tj->ij', left_rows, right_rows, preferred_element_type=F32)  28 us
    dot_general x7, matrix products, times_trans(): return jnp.einsum('tj,ij->ti', rows_mat, weight, preferred_element_type=F32)  24.9 us
    unnamed x110, local copies, waits for them, and re-layouts  22.7 us
    reshape x11, local copies, waits for them, and re-layouts, split_heads(): return matrix.reshape(-1, length, HEADS, HEAD_DIM)  19 us

profile of v1, /device:TPU:0, one launch (start us, length us, event | category | flops | bytes accessed | tf_op | source)
XLA Modules:
  0.0 563.0 jit_solution(17559448265017856260)
XLA Ops:
  3.0 179.9 %gather_parameters.1 = (bf16[4,2,2,2,16,128]{5,4,3,2,1,0:T(8,128)(2,1)}, bf16[4,2,2,2,32,3072]{5,4,3,2,1,0:T(8,128)(2,1)}, bf16[4,2,2,2,32,1024]{5,4,3,2,1,0:T(8...) custom-call(bf16[16,128]{1,0:T(8,128)(2,1)} %maximum_maximum_fusion., ...), custom_call_target="tpu_custom_call" | custom-call | tf_op jit(solution)/shard_map/gather_parameters/pallas_call | solution.py:155
  184.8 4.7 convolution_bitcast_fusion.1
  189.5 2.0 copy-done.24
  191.7 1.6 reshape.335
  193.4 4.7 convolution_bitcast_fusion
  202.7 1.8 fusion.148
  208.9 2.5 reshape.346
  211.4 2.8 copy.56
  214.1 2.7 slice.173
  216.8 2.1 reshape.338
  219.0 2.7 fusion.9
  227.6 2.5 convolution_add_fusion
  230.2 3.0 fusion.151
  235.4 7.6 %fusion.152 = (bf16[4096]{0:T(1024)(128)(2,1)S(1)}, bf16[256,4096]{1,0:T(8,128)(2,1)S(1)}) fusion(f32[256,4096]{1,0:T(8,128)S(1)} %convolution_add_fusion, bf16[4096,1024]{1,0:T(8,128)(2,1)} %bitcast.247, f32[256,1024]{1,0:T(8,128)S(1)} %get-tuple-element.59), kind=kOutput, calls=%fused_computation.222 | convolution fusion | flops 2168713216 | bytes 15736832 | tf_op jit(solution)/shard_map/tj,ij->ti/dot_general | solution.py:373
  243.0 2.9 fusion.74
  248.8 2.5 reshape.347
  251.3 2.8 copy.61
  254.1 4.1 fusion.87
  258.2 28.1 %convert_reduce_fusion.5 = (bf16[16,64]{1,0:T(8,128)(2,1)S(1)}, bf16[2,128,16,64]{1,3,2,0:T(8,128)(2,1)}) fusion(f32[2,16,128,256]{3,2,1,0:T(8,128)} %fusion.87, f32[2,16,128]{2,1,0:T(8,128)S(1)} %log_add_fusion, f32[2,16,128,256]{3,2,1,0:T(8,128)} %copy-done.2, pred[2,256]{1,0:T(4,128)(4,1)S(1)} %iota_compare_fusion.1, bf16[2,256,16,64]{1,0,3,2:T(2,128)(2,1)} %reshape.338), kind=kOutput, calls=%fused_computation.105 | convolution fusion | flops 146541824 | bytes 9980416 | tf_op jit(solution)/shard_map/shqk,skhe->sqhe/dot_general | solution.py:448
  286.3 1.6 copy.64
  287.9 3.2 fusion.75
  293.2 1.6 reshape.348
  294.9 2.0 copy.66
  296.9 1.8 fusion.105
  298.7 5.4 convert_reduce_fusion.8
  304.1 1.6 copy.70
  306.6 5.4 fusion.64
  312.0 1.7 copy.73
  314.6 2.8 convert_reduce_fusion.7
  319.1 5.5 fusion.56
  324.7 29.7 %fusion.39 = bf16[2,256,16,64]{1,3,2,0:T(8,128)(2,1)} fusion(bf16[2,128,16,64]{1,3,2,0:T(8,128)(2,1)} %copy.56, f32[2,16,128,256]{3,2,1,0:T(8,128)} %fusion.87, f32[2,16,128,256]{3,2,1,0:T(8,128)} %copy-done.2, f32[2,16,128]{2,1,0:T(8,128)S(1)} %log_add_fusion, pred[2,256]{1,0:T(4,128)(4,1)S(1)} %iota_compare_fusion.1), kind=kOutput, calls=%fused_computation.60 | convolution fusion | flops 146280704 | bytes 9978368 | tf_op jit(solution)/shard_map/shqk,sqhe->skhe/dot_general | solution.py:451
  354.4 2.5 copy.78
  357.2 1.6 convert_reduce_fusion
  361.1 3.4 convolution_convert_fusion.8
  365.7 6.1 %convolution_convert_fusion.2 = bf16[3072,1024]{0,1:T(8,128)(2,1)} fusion(bf16[256,3072]{0,1:T(8,128)(2,1)} %copy-done.12, bf16[256,1024]{1,0:T(8,128)(2,1)} %param.16), kind=kOutput, calls=%fused_computation.6 | convolution fusion | flops 1613758464 | bytes 8388608 | tf_op jit(solution)/shard_map/ti,tj->ij/dot_general | solution.py:377
  371.8 2.0 convolution_convert_fusion.6
  373.8 2.1 convolution_convert_fusion.5
  375.9 4.5 convolution_convert_fusion.3
  380.4 2.0 convolution_convert_fusion.4
  382.5 6.0 %convolution_convert_fusion.1 = bf16[1024,4096]{1,0:T(8,128)(2,1)} fusion(bf16[256,4096]{1,0:T(8,128)(2,1)S(1)} %copy-done.27, f32[256,1024]{1,0:T(8,128)S(1)} %get-tuple-element.93, f32[1024]{0:T(1024)S(1)} %bitcast.214, f32[1024]{0:T(1024)S(1)} %bitcast.208, f32[256]{0:T(256)S(1)} %add_rsqrt_fusion.1, f32[256]{0:T(256)S(1)} %broadcast_multiply_fusion.7), kind=kOutput, calls=%fused_computation.3 | convolution fusion | flops 2152988672 | bytes 11544576 | tf_op jit(solution)/shard_map/ti,tj->ij/dot_general | solution.py:377
  388.5 5.2 convolution_convert_fusion
  393.7 153.2 %scatter_gradients.1 = (f32[16,128]{1,0:T(8,128)}, f32[32,3072]{1,0:T(8,128)}, f32[32,1024]{1,0:T(8,128)}, f32[32,1024]{1,0:T(8,128)}, f32[32,2048]{1,0:T(8,128)...) custom-call(bf16[4,2,2,2,16,128]{5,4,3,2,1,0:T(8,128)(2,1)} %maximum_maximum_fusion.refs_0_, ...), custom_call_target="tpu_custom_call" | custom-call | tf_op jit(solution)/shard_map/scatter_gradients/pallas_call | solution.py:337
  550.8 1.8 copy.173
  552.6 1.6 copy.174
  555.7 1.7 copy.176
  557.4 1.6 copy.177
  559.0 1.9 copy.178
  560.8 1.9 copy.179
  (179 shorter events, 39.1 us)
Async XLA Ops:
  0.6 184.1 %copy-start = (bf16[512,1024]{1,0:T(8,128)(2,1)S(1)}, bf16[512,1024]{1,0:T(8,128)(2,1)}, u32[]{:S(2)}) copy-start(bf16[512,1024]{1,0:T(8,128)(2,1)} %param.17) | copy-start | bytes 3145732
  189.4 2.1 copy-start.24
  189.4 3.9 copy-start.41
  189.5 3.9 copy-start.28
  198.1 1.6 copy-start.25
  198.1 4.3 copy-start.42
  199.9 5.0 copy-start.21
  202.4 2.9 copy-start.38
  202.6 3.3 copy-start.8
  202.6 3.3 copy-start.29
  204.4 2.3 copy-start.1
  205.3 2.0 copy-start.40
  205.9 3.0 copy-start.13
  207.3 9.5 %copy-start.17 = (bf16[256,1024]{1,0:T(8,128)(2,1)}, bf16[256,1024]{1,0:T(8,128)(2,1)S(1)}, u32[]{:S(2)}) copy-start(bf16[256,1024]{1,0:T(8,128)(2,1)S(1)} %add_convert_fusion.1) | copy-start | bytes 1572868
  219.0 4.2 copy-start.23
  221.7 3.1 copy-start.2
  221.7 5.6 slice-start
  223.2 3.0 copy-start.10
  223.2 2.9 copy-start.18
  223.2 4.4 slice-start.1
  226.1 4.0 slice-start.2
  227.6 2.6 slice-start.3
  230.2 5.2 copy-start.43
  230.2 3.2 copy-start.30
  235.4 7.6 %copy-start.34 = (f32[256,1024]{1,0:T(8,128)}, f32[256,1024]{1,0:T(8,128)S(1)}, u32[]{:S(2)}) copy-start(f32[256,1024]{1,0:T(8,128)S(1)} %get-tuple-element.59) | copy-start | bytes 3145732
  243.0 2.9 copy-start.26
  246.3 1.0 copy-start.4
  287.8 3.6 copy-start.31
  287.8 4.6 copy-start.9
  291.5 1.0 copy-start.6
  291.5 5.4 copy-start.22
  296.9 8.8 %copy-start.20 = (bf16[2,128,16,64]{1,3,2,0:T(8,128)(2,1)}, bf16[2,128,16,64]{1,3,2,0:T(8,128)(2,1)S(1)}, u32[]{:S(2)}) copy-start(bf16[2,128,16,64]{1,3,2,0:T(8,128)(2,1)S(1)} %copy.66) | copy-start | bytes 1572868
  312.0 7.2 %copy-start.7 = (f32[256,1024]{1,0:T(8,128)S(1)}, f32[256,1024]{1,0:T(8,128)}, u32[]{:S(2)}) copy-start(f32[256,1024]{1,0:T(8,128)} %copy-done.6) | copy-start | bytes 3145732
  314.6 3.3 copy-start.11
  318.0 1.2 copy-start.12
  354.4 2.8 copy-start.3
  354.4 2.8 copy-start.33
  358.9 2.2 copy-start.39
  361.1 3.4 copy-start.36
  365.7 6.1 %copy-start.14 = (bf16[2,128,16,64]{1,0,3,2:T(2,128)(2,1)S(1)}, bf16[2,128,16,64]{1,0,3,2:T(2,128)(2,1)}, u32[]{:S(2)}) copy-start(bf16[2,128,16,64]{1,0,3,2:T(2,128)(2,1)} %copy-done.13) | copy-start | bytes 1572868
  365.7 8.2 %copy-start.19 = (bf16[256,1024]{1,0:T(8,128)(2,1)S(1)}, bf16[256,1024]{1,0:T(8,128)(2,1)}, u32[]{:S(2)}) copy-start(bf16[256,1024]{1,0:T(8,128)(2,1)} %copy-done.17) | copy-start | bytes 1572868
  365.7 8.2 %copy-start.32 = (bf16[2,128,16,64]{1,0,3,2:T(2,128)(2,1)S(1)}, bf16[2,128,16,64]{1,0,3,2:T(2,128)(2,1)}, u32[]{:S(2)}) copy-start(bf16[2,128,16,64]{1,0,3,2:T(2,128)(2,1)} %copy-done.31) | copy-start | bytes 1572868
  371.8 4.1 copy-start.37
  375.9 4.5 copy-start.5
  375.9 4.5 copy-start.16
  380.4 2.0 copy-start.27
  382.5 6.0 %copy-start.35 = (f32[256,1024]{1,0:T(8,128)S(1)}, f32[256,1024]{1,0:T(8,128)}, u32[]{:S(2)}) copy-start(f32[256,1024]{1,0:T(8,128)} %copy-done.34) | copy-start | bytes 3145732
  382.5 6.0 %copy-start.44 = (f32[256,4096]{1,0:T(8,128)S(1)}, f32[256,4096]{1,0:T(8,128)}, u32[]{:S(2)}) copy-start(f32[256,4096]{1,0:T(8,128)} %copy-done.43) | copy-start | bytes 12582916
  (1 other events, 0.8 us)
